TPU v7x, 1024 devices: a whole 8x8x8 slice. The times are simulated.
1024 devices in a mesh: dp: 64 (over z, x), expert: 16 (over y, core).
Axes of the slice: x: 8, y: 8, z: 8, core: 2. Of those that a mesh axis runs over, the one named last changes fastest.
Arguments:
- tokens: bfloat16 [131072, 2048], P(('dp', 'expert')), may hold values from -6 to 6
- expert_index: int32 [131072, 2], P(('dp', 'expert')), may hold values from 0 to 15, all different within a row; in each aligned block of 128 rows (0 to 127, 128 to 255, ...) at most 20 rows name the same one
- gate_weights: bfloat16 [131072, 2], P(('dp', 'expert')), may hold values from 0.049804688 to 1
- cotangent: bfloat16 [131072, 2048], P(('dp', 'expert')), may hold values from -24 to 24
- w_gate: bfloat16 [16, 2048, 384], P('expert'), may hold values from -0.125 to 0.125
- w_up: bfloat16 [16, 2048, 384], P('expert'), may hold values from -0.125 to 0.125
- w_down: bfloat16 [16, 384, 2048], P('expert'), may hold values from -0.3125 to 0.3125
Outputs:
- token_grad: bfloat16 [131072, 2048], P(('dp', 'expert'))
- down_grad: float32 [16, 384, 2048], P('expert', None, 'dp')
Inputs may be any that keep to these rules, and one draw needn't show every extreme that they name: `expert_index`: the 2 experts of a token differ. Within each device's aligned block of 128 tokens no expert is named more than 20 times, and in every draw some block names some expert exactly 20 times.
All inputs are finite; a program needn't handle non-finite values.
Results may differ from a plain program's by a relative error of at most 0.0065.
Values may be sent and summed in bfloat16 or wider, within the bound.
A program may use at most 32 MiB of HBM per device.

v0:
```python
import jax
import jax.numpy as jnp
from jax import lax
from jax.sharding import PartitionSpec as P


def per_device(tokens, expert_index, gate_weights, cotangent, w_gate, w_up, w_down):
    expert_count = lax.axis_size("expert")
    tok_rows, model_width = tokens.shape
    top_count = expert_index.shape[1]
    slot_cap = tok_rows * top_count * 5 // (4 * expert_count)
    pair_count = tok_rows * top_count
    slot_count = expert_count * slot_cap
    chosen = expert_index.reshape(pair_count)
    matches = (chosen[:, None] == jnp.arange(expert_count, dtype=jnp.int32)[None, :]).astype(
        jnp.int32
    )
    earlier = jnp.cumsum(matches, axis=0) - matches
    position = jnp.sum(earlier * matches, axis=1)
    slot_target = chosen * slot_cap + position
    slot_ids = jnp.arange(slot_count, dtype=jnp.int32)
    pair_table = (slot_ids[:, None] == slot_target[None, :]).astype(jnp.bfloat16)
    token_table = jnp.sum(pair_table.reshape(slot_count, tok_rows, top_count), axis=2)
    gate_matrix = w_gate[0]
    up_matrix = w_up[0]
    down_matrix = w_down[0]
    outgoing = jnp.dot(token_table, tokens, preferred_element_type=jnp.float32).astype(jnp.bfloat16)
    outgoing = outgoing.reshape(expert_count, slot_cap, model_width)
    received = lax.all_to_all(outgoing, "expert", split_axis=0, concat_axis=0, tiled=True).reshape(
        slot_count, model_width
    )
    gate_pre = jnp.dot(received, gate_matrix, preferred_element_type=jnp.float32)
    up_pre = jnp.dot(received, up_matrix, preferred_element_type=jnp.float32)
    sigmoid_gate = jax.nn.sigmoid(gate_pre)
    silu_gate = gate_pre * sigmoid_gate
    hidden = (silu_gate * up_pre).astype(jnp.bfloat16)
    scaled_pairs = (
        gate_weights.astype(jnp.float32)[:, :, None] * cotangent.astype(jnp.float32)[:, None, :]
    )
    scaled_pairs = scaled_pairs.astype(jnp.bfloat16).reshape(pair_count, model_width)
    scaled_out = jnp.dot(pair_table, scaled_pairs, preferred_element_type=jnp.float32).astype(
        jnp.bfloat16
    )
    scaled_out = scaled_out.reshape(expert_count, slot_cap, model_width)
    scaled = lax.all_to_all(scaled_out, "expert", split_axis=0, concat_axis=0, tiled=True)
    scaled = scaled.reshape(slot_count, model_width)
    last_dims = (((1,), (1,)), ((), ()))
    first_dims = (((0,), (0,)), ((), ()))
    hidden_grad = lax.dot_general(
        scaled, down_matrix, last_dims, preferred_element_type=jnp.float32
    )
    gate_grad = (
        hidden_grad * up_pre * sigmoid_gate * (1.0 + gate_pre * (1.0 - sigmoid_gate))
    ).astype(jnp.bfloat16)
    up_grad = (hidden_grad * silu_gate).astype(jnp.bfloat16)
    pair_grad = lax.dot_general(
        gate_grad, gate_matrix, last_dims, preferred_element_type=jnp.float32
    ) + lax.dot_general(up_grad, up_matrix, last_dims, preferred_element_type=jnp.float32)
    pair_grad = pair_grad.astype(jnp.bfloat16).reshape(expert_count, slot_cap, model_width)
    returned = lax.all_to_all(pair_grad, "expert", split_axis=0, concat_axis=0, tiled=True).reshape(
        slot_count, model_width
    )
    token_grad = lax.dot_general(
        token_table, returned, first_dims, preferred_element_type=jnp.float32
    )
    token_grad = token_grad.astype(jnp.bfloat16)
    down_term = lax.dot_general(hidden, scaled, first_dims, preferred_element_type=jnp.float32)
    down_grad = lax.psum_scatter(down_term[None], "dp", scatter_dimension=2, tiled=True)
    return (token_grad, down_grad)


def solution(mesh):
    in_specs = (
        P(("dp", "expert"), None),
        P(("dp", "expert"), None),
        P(("dp", "expert"), None),
        P(("dp", "expert"), None),
        P("expert", None, None),
        P("expert", None, None),
        P("expert", None, None),
    )
    out_specs = (P(("dp", "expert"), None), P("expert", None, "dp"))
    return jax.shard_map(
        per_device, mesh=mesh, in_specs=in_specs, out_specs=out_specs, check_vma=False
    )
```

profile of v0, /device:TPU:4, one launch (start us, length us, event | category | flops | bytes accessed | tf_op | source)
XLA Modules:
  0.0 316.2 jit_solution(2278821803602210557)
XLA Ops:
  7.2 0.0 copy-start
  7.2 0.9 copy.35
  8.1 0.1 eq.50
  8.2 0.1 eq.46
  8.4 0.6 reduce-window.6
  9.0 0.2 slice_reduce_fusion
  9.2 0.1 fusion.20
  9.3 0.1 reduce_sum.24
  9.4 0.1 copy.38
  9.5 0.7 multiply_add_fusion.1
  10.3 1.5 convolution_convert_fusion
  11.8 1.3 reshape.68
  13.1 7.7 %all-to-all-start.1 = ((bf16[16,20,2048]{2,1,0:T(8,128)(2,1)}), bf16[16,20,2048]{2,1,0:T(8,128)(2,1)S(1)}, u32[]{:S(2)}, u32[]{:S(2)}) async-start(bf16[16,20,2048]{2,1,0:T(8,128)(2,1)} %reshape.68), calls=%async_computation.1 | async-start | bytes 3145728 | tf_op jit(solution)/shard_map/all_to_all | solution.py:29
  20.8 3.4 %mul.67 = f32[128,2,2048]{2,1,0:T(2,128)} broadcast(bf16[128,2048]{1,0:T(8,128)(2,1)} %param.10), dimensions={0,2} | broadcast | bytes 2621440 | tf_op jit(solution)/shard_map/mul | solution.py:38
  24.2 0.0 copy-start.6
  24.2 3.7 %mul.68 = f32[256,2048]{1,0:T(8,128)} reshape(f32[128,2,2048]{2,1,0:T(2,128)} %mul.67) | data formatting | bytes 4194304 | tf_op jit(solution)/shard_map/mul | solution.py:38
  27.9 0.0 copy-done.6
  27.9 0.1 copy.39
  28.0 0.1 reshape.72
  28.2 3.2 %convolution_convert_fusion.1 = bf16[320,2048]{1,0:T(8,128)(2,1)} fusion(f32[256,2048]{1,0:T(8,128)} %mul.68, f32[256]{0:T(256)S(1)} %reshape.72, s32[256]{0:T(256)S(1)} %multiply_add_fusion), kind=kOutput, calls=%fused_computation.4 | convolution fusion | flops 337330176 | bytes 3409920 | tf_op jit(solution)/shard_map/dot_general | solution.py:41
  31.4 3.2 %reshape.66 = bf16[16,20,2048]{2,1,0:T(8,128)(2,1)} reshape(bf16[320,2048]{1,0:T(8,128)(2,1)} %convolution_convert_fusion.1) | data formatting | bytes 2621440 | tf_op jit(solution)/shard_map/reshape | solution.py:44
  34.6 24.0 %all-to-all-done.1 = bf16[16,20,2048]{2,1,0:T(8,128)(2,1)S(1)} async-done(((bf16[16,20,2048]{2,1,0:T(8,128)(2,1)}), bf16[16,20,2048]{2,1,0:T(8,128)(2,1)S(1)}, u32[]{:S(2)}, u32[]{:S(2)}) %all-to-all-start.1) | async-done | bytes 1310752 | tf_op jit(solution)/shard_map/all_to_all | solution.py:29
  58.6 4.9 %all-to-all-start = ((bf16[16,20,2048]{2,1,0:T(8,128)(2,1)}), bf16[16,20,2048]{2,1,0:T(8,128)(2,1)}, u32[]{:S(2)}, u32[]{:S(2)}) async-start(bf16[16,20,2048]{2,1,0:T(8,128)(2,1)} %reshape.66), calls=%async_computation | async-start | bytes 3145728 | tf_op jit(solution)/shard_map/all_to_all | solution.py:45
  63.5 0.0 all-reduce.3.cloned.1.call-start
  63.6 1.2 reshape.69
  64.8 0.0 copy-done
  64.8 0.0 copy-start.2
  64.8 0.0 copy-start.4
  64.8 2.3 fusion.3
  67.1 0.0 copy-done.2
  67.1 0.0 copy-done.4
  67.1 0.8 fusion.6
  68.0 33.5 %all-to-all-done = bf16[16,20,2048]{2,1,0:T(8,128)(2,1)} async-done(((bf16[16,20,2048]{2,1,0:T(8,128)(2,1)}), bf16[16,20,2048]{2,1,0:T(8,128)(2,1)}, u32[]{:S(2)}, u32[]{:S(2)}) %all-to-all-start) | async-done | bytes 1310752 | tf_op jit(solution)/shard_map/all_to_all | solution.py:45
  101.4 3.3 %reshape.67 = bf16[320,2048]{1,0:T(8,128)(2,1)} reshape(bf16[16,20,2048]{2,1,0:T(8,128)(2,1)} %all-to-all-done) | data formatting | bytes 2621440 | tf_op jit(solution)/shard_map/reshape | solution.py:46
  104.7 0.0 copy-start.5
  104.7 2.8 fusion.8
  107.5 0.0 copy-done.5
  107.5 0.0 copy-start.1
  107.5 2.8 convolution_bitcast_fusion
  110.3 8.5 %copy.40 = f32[1,384,2048]{1,0,2:T(1,128)} copy(f32[1,384,2048]{2,1,0:T(8,128)} %convolution_bitcast_fusion) | data formatting | bytes 6291456 | tf_op jit(solution)/shard_map/broadcast_in_dim | solution.py:68
  118.8 0.0 all-reduce.3.cloned.1.call-update
  118.8 0.0 copy-done.1
  118.8 0.0 copy-start.3
  118.8 0.9 fusion.1
  119.8 0.5 copy-done.3
  120.2 1.9 fusion
  122.2 1.3 reshape.70
  123.5 4.8 %all-to-all-start.2 = ((bf16[16,20,2048]{2,1,0:T(8,128)(2,1)}), bf16[16,20,2048]{2,1,0:T(8,128)(2,1)S(1)}, u32[]{:S(2)}, u32[]{:S(2)}) async-start(bf16[16,20,2048]{2,1,0:T(8,128)(2,1)} %reshape.70), calls=%async_computation.2 | async-start | bytes 3145728 | tf_op jit(solution)/shard_map/all_to_all | solution.py:60
  128.3 1.3 dynamic-slice
  130.2 35.9 %all-to-all-done.2 = bf16[16,20,2048]{2,1,0:T(8,128)(2,1)S(1)} async-done(((bf16[16,20,2048]{2,1,0:T(8,128)(2,1)}), bf16[16,20,2048]{2,1,0:T(8,128)(2,1)S(1)}, u32[]{:S(2)}, u32[]{:S(2)}) %all-to-all-start.2) | async-done | bytes 1310752 | tf_op jit(solution)/shard_map/all_to_all | solution.py:60
  166.2 1.2 reshape.71
  167.4 2.6 convolution_convert_fusion.2
  170.0 138.0 %all-reduce.3.cloned.1.call-done = f32[1,384,2048]{1,0,2:T(1,128)} async-done(((f32[1,384,2048]{1,0,2:T(1,128)}), f32[1,384,2048]{1,0,2:T(1,128)}) %all-reduce.3.cloned.1.call-update) | async-done | bytes 3145744
  308.0 0.8 constant_dynamic-slice_fusion
  308.8 0.6 copy.41
  (5 shorter events, 0.1 us)
Async XLA Ops:
  7.2 57.6 %copy-start = (bf16[1,2048,384]{2,1,0:T(8,128)(2,1)S(1)}, bf16[1,2048,384]{2,1,0:T(8,128)(2,1)}, u32[]{:S(2)}) copy-start(bf16[1,2048,384]{2,1,0:T(8,128)(2,1)} %param.11) | copy-start | bytes 4718596
  13.1 45.5 %all-to-all-start.1 = ((bf16[16,20,2048]{2,1,0:T(8,128)(2,1)}), bf16[16,20,2048]{2,1,0:T(8,128)(2,1)S(1)}, u32[]{:S(2)}, u32[]{:S(2)}) async-start(bf16[16,20,2048]{2,1,0:T(8,128)(2,1)} %reshape.68), calls=%async_computation.1 | async-start | bytes 3145728 | tf_op jit(solution)/shard_map/all_to_all | solution.py:29
  24.2 3.7 %copy-start.6 = (bf16[128,2]{0,1:T(2,128)(2,1)S(1)}, bf16[128,2]{0,1:T(2,128)(2,1)}, u32[]{:S(2)}) copy-start(bf16[128,2]{0,1:T(2,128)(2,1)} %param.9) | copy-start | bytes 1540
  58.6 42.8 %all-to-all-start = ((bf16[16,20,2048]{2,1,0:T(8,128)(2,1)}), bf16[16,20,2048]{2,1,0:T(8,128)(2,1)}, u32[]{:S(2)}, u32[]{:S(2)}) async-start(bf16[16,20,2048]{2,1,0:T(8,128)(2,1)} %reshape.66), calls=%async_computation | async-start | bytes 3145728 | tf_op jit(solution)/shard_map/all_to_all | solution.py:45
  63.5 244.4 %all-reduce.3.cloned.1.call-start = ((), (), s32[]{:S(2)}) async-start(), calls=%async_computation.3 | async-start | bytes 6291456
  64.8 2.3 copy-start.2
  64.8 2.3 copy-start.4
  104.7 2.8 copy-start.5
  107.5 11.3 %copy-start.1 = (f32[320,384]{1,0:T(8,128)}, f32[320,384]{1,0:T(8,128)S(1)}, u32[]{:S(2)}) copy-start(f32[320,384]{1,0:T(8,128)S(1)} %fusion.8) | copy-start | bytes 1474564
  118.8 1.4 copy-start.3
  123.5 42.7 %all-to-all-start.2 = ((bf16[16,20,2048]{2,1,0:T(8,128)(2,1)}), bf16[16,20,2048]{2,1,0:T(8,128)(2,1)S(1)}, u32[]{:S(2)}, u32[]{:S(2)}) async-start(bf16[16,20,2048]{2,1,0:T(8,128)(2,1)} %reshape.70), calls=%async_computation.2 | async-start | bytes 3145728 | tf_op jit(solution)/shard_map/all_to_all | solution.py:60
Sparse Core Ops, SparseCore 0:
  118.9 188.9 all-reduce.2
where the time goes:
time: 317 us; the launch traced here: 316 us
  waiting for transfers between devices  231 us (73%)
  local copies, waits for them, and re-layouts  32.2 us (10%)
  matrix products  18.9 us (6%)
  starting transfers between devices  17.4 us (5%)
  between operations  14.9 us (5%)
    unnamed x2, waiting for transfers between devices  138 us
    all_to_all x1, waiting for transfers between devices, per_device(): lax.all_to_all(pair_grad, 'expert', split_axis=0, concat_axis=0, tiled=True)  35.9 us
    all_to_all x1, waiting for transfers between devices, per_device(): lax.all_to_all(scaled_out, 'expert', split_axis=0, concat_axis=0, tiled=T...  33.5 us
    all_to_all x1, waiting for transfers between devices, per_device(): lax.all_to_all(outgoing, 'expert', split_axis=0, concat_axis=0, tiled=True)  24 us
    broadcast_in_dim x1, local copies, waits for them, and re-layouts, per_device(): down_term[None]  8.5 us
    all_to_all x1, starting transfers between devices, per_device(): lax.all_to_all(outgoing, 'expert', split_axis=0, concat_axis=0, tiled=True)  7.66 us
    mul x4, local copies, waits for them, and re-layouts, per_device(): gate_weights.astype(jnp.float32)[:, :, None]  7.37 us
  transfers between devices with their start and end apart: 4, of which 4 were waited for; matrix products, arithmetic and copies ran while one was open for 9% of the time, Pallas kernels for 0%

commit v1 on v0

v1 whole, which is shorter than its diff:
```python
import functools

import jax
import jax.numpy as jnp
from jax import lax
from jax.experimental import pallas as pl
from jax.experimental.pallas import tpu as pltpu
from jax.sharding import PartitionSpec as P

MESH = pl.DeviceIdType.MESH
F32 = jnp.float32
BF16 = jnp.bfloat16

SIDE = 8
PEERS = 16
SLOTS = 20
MAIN = 16
SPARE = SLOTS - MAIN
FOLD = MAIN // SPARE
GROUP = 4
CHUNKS = PEERS // GROUP
GM = GROUP * MAIN
GS = GROUP * SPARE
GROWS = GM + GS

NT = (((1,), (1,)), ((), ()))
TN = (((0,), (0,)), ((), ()))


def offsets_of(slot):
    pair = slot // 2
    far = 4 - (pair + 1) // 2
    return far * (2 * (pair & 1) - 1), (slot + 1) & 1


def dot(a, b, dims=(((1,), (0,)), ((), ()))):
    return lax.dot_general(a, b, dims, preferred_element_type=F32)


def body(
    ei_ref, gw_ref, tok_hbm, cot_hbm, wg_hbm, wu_hbm, wd_hbm,
    tg_ref, dg_ref,
    tok, cot, wgu, wd, x_out, x_in, c_out, c_in, r_out, r_in,
    t_main, t_spare, xs, pre, scaled, hidden,
    dt_a, dt_b, r_a, r_b, s_a, s_b, q_a, q_b,
    load_sem, xs_sem, xr_sem, cs_sem, cr_sem, rs_sem, rr_sem,
    a1s, a1r, b1s, b1r, a2s, a2r, b2s, b2r,
):
    width = tok.shape[1]
    rows = tok.shape[0]
    ff = wd.shape[0]
    fold = width // FOLD
    part = width // SIDE
    dp = lax.axis_index("dp")
    ex = lax.axis_index("expert")
    z, x = dp // SIDE, dp % SIDE
    y, core = ex // 2, ex % 2

    loads = [
        pltpu.make_async_copy(tok_hbm, tok, load_sem.at[0]),
        pltpu.make_async_copy(cot_hbm, cot, load_sem.at[1]),
        pltpu.make_async_copy(wg_hbm, wgu.at[:, pl.ds(0, ff)], load_sem.at[2]),
        pltpu.make_async_copy(wu_hbm, wgu.at[:, pl.ds(ff, ff)], load_sem.at[3]),
        pltpu.make_async_copy(wd_hbm, wd, load_sem.at[4]),
    ]
    for load in loads:
        load.start()

    def target(slot, way):
        along, other = offsets_of(slot)
        return (dp, ((y + way * along) & (SIDE - 1)) * 2 + ((core + other) & 1))

    def x_peer(k):
        return (z * SIDE + ((x + k) & (SIDE - 1)), ex)

    def z_peer(k):
        return (((z + k) & (SIDE - 1)) * SIDE + x, ex)

    barrier = pltpu.get_barrier_semaphore()
    for slot in range(PEERS - 1):
        pl.semaphore_signal(barrier, inc=1, device_id=target(slot, 1), device_id_type=MESH)
    for k in range(1, SIDE):
        pl.semaphore_signal(barrier, inc=1, device_id=x_peer(k), device_id_type=MESH)
        pl.semaphore_signal(barrier, inc=1, device_id=z_peer(k), device_id_type=MESH)

    lane_e = lax.broadcasted_iota(jnp.int32, (rows, PEERS), 1)
    first = (ei_ref[:, 0:1] == lane_e).astype(F32)
    second = (ei_ref[:, 1:2] == lane_e).astype(F32)
    chosen = (first + second).astype(BF16)
    gates = gw_ref[...].astype(F32)
    gates = (first * gates[:, 0:1] + second * gates[:, 1:2]).astype(BF16)
    before = lax.broadcasted_iota(jnp.int32, (rows, rows), 1) < lax.broadcasted_iota(
        jnp.int32, (rows, rows), 0
    )
    place = dot(before.astype(F32).astype(BF16), chosen).astype(BF16)

    def expert_at(block):
        along, other = offsets_of(block)
        return ((y + along) & (SIDE - 1)) * 2 + ((core + other) & 1)

    nrow = PEERS * MAIN
    down_i = lax.broadcasted_iota(jnp.int32, (nrow, PEERS), 0)
    pick = (
        expert_at(down_i // MAIN) == lax.broadcasted_iota(jnp.int32, (nrow, PEERS), 1)
    ).astype(F32).astype(BF16)
    named = dot(pick, chosen, NT) > 0.5
    at = dot(pick, place, NT).astype(jnp.int32)
    gate_of = dot(pick, gates, NT)
    row_i = lax.broadcasted_iota(jnp.int32, (nrow, rows), 0)
    hit_main = jnp.where(named & (at == (row_i & (MAIN - 1))), 1.0, 0.0)
    hit_spare = jnp.where(named & (at == MAIN + (row_i & (SPARE - 1))), 1.0, 0.0)
    scale_main = jnp.sum(hit_main * gate_of, axis=1, keepdims=True)
    scale_spare = jnp.sum(hit_spare * gate_of, axis=1, keepdims=True)
    piece_i = (row_i & (MAIN - 1)) // SPARE
    take_main = hit_main.astype(BF16)
    take_spare = [
        jnp.where(piece_i == g, hit_spare, 0.0).astype(BF16) for g in range(FOLD)
    ]
    named_t = dot(chosen, pick, NT) > 0.5
    at_t = dot(place, pick, NT).astype(jnp.int32)
    col_i = lax.broadcasted_iota(jnp.int32, (rows, nrow), 1)
    t_main[...] = jnp.where(named_t & (at_t == (col_i & (MAIN - 1))), 1.0, 0.0).astype(BF16)
    t_spare[...] = jnp.where(
        named_t & (at_t == MAIN + (col_i & (SPARE - 1))), 1.0, 0.0
    ).astype(BF16)

    def gather(source, out, scales):
        for g in range(FOLD):
            cols = slice(g * fold, (g + 1) * fold)
            got = dot(take_main, source[:, cols])
            if scales is not None:
                got = got * scales[0]
            out[:, :, cols] = got.astype(BF16).reshape(PEERS, MAIN, fold)
        got = dot(take_spare[0], source[:, 0:fold])
        for g in range(1, FOLD):
            got = got + dot(take_spare[g], source[:, g * fold : (g + 1) * fold])
        if scales is not None:
            got = got * scales[1]
        out[:, :, width:] = got.astype(BF16).reshape(PEERS, MAIN, fold)

    def move(slot, way, out, into, send, recv):
        return pltpu.make_async_remote_copy(
            src_ref=out.at[slot],
            dst_ref=into.at[slot],
            send_sem=send.at[slot],
            recv_sem=recv.at[slot],
            device_id=target(slot, way),
            device_id_type=MESH,
        )

    own = PEERS - 1
    loads[0].wait()
    gather(tok, x_out, None)
    pl.semaphore_wait(barrier, PEERS - 1 + 2 * (SIDE - 1))
    for slot in range(PEERS - 1):
        move(slot, 1, x_out, x_in, xs_sem, xr_sem).start()
    loads[1].wait()
    gather(cot, c_out, (scale_main, scale_spare))
    for slot in range(PEERS - 1):
        move(slot, 1, c_out, c_in, cs_sem, cr_sem).start()
    x_in[own] = x_out[own]
    c_in[own] = c_out[own]

    big_i = lax.broadcasted_iota(jnp.int32, (GS, GM), 1)
    small_i = lax.broadcasted_iota(jnp.int32, (GS, GM), 0)
    big_t = lax.broadcasted_iota(jnp.int32, (GM, GS), 0)
    small_t = lax.broadcasted_iota(jnp.int32, (GM, GS), 1)

    def unfold(g):
        want = (small_i // SPARE) * MAIN + g * SPARE + (small_i & (SPARE - 1))
        return jnp.where(big_i == want, 1.0, 0.0).astype(BF16)

    def refold(g):
        want = (small_t // SPARE) * MAIN + g * SPARE + (small_t & (SPARE - 1))
        return jnp.where(big_t == want, 1.0, 0.0).astype(BF16)

    def wait_block(slot, way, out, into, send, recv):
        @pl.when(slot < own)
        def _():
            move(slot, way, out, into, send, recv).wait_recv()

    def unpack(into, chunk, dest, base):
        blocks = into.at[pl.ds(chunk * GROUP, GROUP)]
        dest[pl.ds(base, GM), :] = blocks[:, :, 0:width].reshape(GM, width)
        spare = blocks[:, :, width:].reshape(GM, fold)
        for g in range(FOLD):
            dest[pl.ds(base + GM, GS), pl.ds(g * fold, fold)] = dot(unfold(g), spare).astype(BF16)

    loads[2].wait()
    loads[3].wait()

    def forward(chunk, carry):
        for b in range(GROUP):
            wait_block(chunk * GROUP + b, 1, x_out, x_in, xs_sem, xr_sem)
        base = pl.multiple_of(chunk * GROWS, GROWS)
        unpack(x_in, chunk, xs, 0)
        both = dot(xs[...], wgu[...])
        pre[pl.ds(base, GROWS), :] = both
        gate = both[:, 0:ff]
        hidden[pl.ds(base, GROWS), :] = (gate * jax.nn.sigmoid(gate) * both[:, ff:]).astype(BF16)
        return carry

    lax.fori_loop(0, CHUNKS, forward, 0)
    loads[4].wait()

    def backward(chunk, carry):
        for b in range(GROUP):
            wait_block(chunk * GROUP + b, 1, c_out, c_in, cs_sem, cr_sem)
        base = pl.multiple_of(chunk * GROWS, GROWS)
        unpack(c_in, chunk, scaled, base)
        back = dot(scaled[pl.ds(base, GROWS), :], wd[...], NT)
        gate = pre[pl.ds(base, GROWS), 0:ff]
        up = pre[pl.ds(base, GROWS), ff:]
        sig = jax.nn.sigmoid(gate)
        gate_grad = (back * up * sig * (1.0 + gate * (1.0 - sig))).astype(BF16)
        up_grad = (back * (gate * sig)).astype(BF16)
        grads = jnp.concatenate([gate_grad, up_grad], axis=1)
        folded = jnp.zeros((GM, fold), F32)
        for g in range(FOLD):
            cols = pl.ds(g * fold, fold)
            pair = dot(grads, wgu[cols, :], NT).astype(BF16)
            r_out[pl.ds(chunk * GROUP, GROUP), :, cols] = pair[0:GM].reshape(GROUP, MAIN, fold)
            folded = folded + dot(refold(g), pair[GM:])
        r_out[pl.ds(chunk * GROUP, GROUP), :, pl.ds(width, fold)] = folded.astype(BF16).reshape(
            GROUP, MAIN, fold
        )
        for b in range(GROUP):
            slot = chunk * GROUP + b

            @pl.when(slot < own)
            def _():
                move(slot, -1, r_out, r_in, rs_sem, rr_sem).start()

        return carry

    lax.fori_loop(0, CHUNKS, backward, 0)
    r_in[own] = r_out[own]

    half = part // (2 * SIDE)

    def outer(zz, carry):
        cols = pl.ds(pl.multiple_of(zz * part, part), part)
        term = dot(scaled[:, cols], hidden[...], TN).astype(BF16).reshape(SIDE, 2, half, ff)
        for xx in range(SIDE):
            dt_a[xx, zz] = term[xx, 0]
        dt_b[zz] = term[:, 1]
        return carry

    lax.fori_loop(0, SIDE, outer, 0)

    def share(k, peer, at_axis, out, into, send, recv):
        return pltpu.make_async_remote_copy(
            src_ref=out.at[(at_axis + k) & (SIDE - 1)],
            dst_ref=into.at[k - 1],
            send_sem=send.at[k - 1],
            recv_sem=recv.at[k - 1],
            device_id=peer(k),
            device_id_type=MESH,
        )

    order = (4, 3, 5, 2, 6, 1, 7)
    for k in order:
        share(k, x_peer, x, dt_a, r_a, a1s, a1r).start()
        share(k, z_peer, z, dt_b, r_b, b1s, b1r).start()
    for k in order:
        share(k, x_peer, x, dt_a, r_a, a1s, a1r).wait_recv()
    total = dt_a[x].astype(F32)
    for k in range(SIDE - 1):
        total = total + r_a[k].astype(F32)
    s_a[...] = total.astype(BF16)
    for k in order:
        share(k, z_peer, z, s_a, q_a, a2s, a2r).start()
    for k in order:
        share(k, z_peer, z, dt_b, r_b, b1s, b1r).wait_recv()
    total = dt_b[z].astype(F32)
    for k in range(SIDE - 1):
        total = total + r_b[k].astype(F32)
    s_b[...] = total.astype(BF16)
    for k in order:
        share(k, x_peer, x, s_b, q_b, b2s, b2r).start()
    for k in order:
        share(k, z_peer, z, s_a, q_a, a2s, a2r).wait_recv()
        share(k, x_peer, x, s_b, q_b, b2s, b2r).wait_recv()
    total = s_a[z].astype(F32)
    for k in range(SIDE - 1):
        total = total + q_a[k].astype(F32)
    dg_ref[0:half, :] = total
    total = s_b[x].astype(F32)
    for k in range(SIDE - 1):
        total = total + q_b[k].astype(F32)
    dg_ref[half:, :] = total

    for slot in range(PEERS - 1):
        move(slot, -1, r_out, r_in, rs_sem, rr_sem).wait_recv()
    col_piece = (lax.broadcasted_iota(jnp.int32, (rows, nrow), 1) & (MAIN - 1)) // SPARE
    spare = r_in[:, :, width:].reshape(nrow, fold)
    for g in range(FOLD):
        cols = slice(g * fold, (g + 1) * fold)
        main = r_in[:, :, cols].reshape(nrow, fold)
        pick_g = jnp.where(col_piece == g, t_spare[...].astype(F32), 0.0).astype(BF16)
        tg_ref[:, cols] = (dot(t_main[...], main) + dot(pick_g, spare)).astype(BF16)

    for slot in range(PEERS - 1):
        move(slot, 1, x_out, x_in, xs_sem, xr_sem).wait_send()
        move(slot, 1, c_out, c_in, cs_sem, cr_sem).wait_send()
        move(slot, -1, r_out, r_in, rs_sem, rr_sem).wait_send()
    for k in order:
        share(k, x_peer, x, dt_a, r_a, a1s, a1r).wait_send()
        share(k, z_peer, z, dt_b, r_b, b1s, b1r).wait_send()
        share(k, z_peer, z, s_a, q_a, a2s, a2r).wait_send()
        share(k, x_peer, x, s_b, q_b, b2s, b2r).wait_send()


def per_device(tokens, expert_index, gate_weights, cotangent, w_gate, w_up, w_down):
    rows, width = tokens.shape
    ff = w_gate.shape[2]
    wide = width + width // FOLD
    half = width // (2 * SIDE * SIDE)
    vmem = pl.BlockSpec(memory_space=pltpu.VMEM)
    hbm = pl.BlockSpec(memory_space=pl.ANY)
    blocks = pltpu.VMEM((PEERS, MAIN, wide), BF16)
    dma = pltpu.SemaphoreType.DMA
    token_grad, down_t = pl.pallas_call(
        body,
        out_shape=(
            jax.ShapeDtypeStruct((rows, width), BF16),
            jax.ShapeDtypeStruct((2 * half, ff), F32),
        ),
        in_specs=[vmem, vmem, hbm, hbm, hbm, hbm, hbm],
        out_specs=(vmem, vmem),
        scratch_shapes=[
            pltpu.VMEM((rows, width), BF16),
            pltpu.VMEM((rows, width), BF16),
            pltpu.VMEM((width, 2 * ff), BF16),
            pltpu.VMEM((ff, width), BF16),
            blocks, blocks, blocks, blocks, blocks, blocks,
            pltpu.VMEM((rows, PEERS * MAIN), BF16),
            pltpu.VMEM((rows, PEERS * MAIN), BF16),
            pltpu.VMEM((GROWS, width), BF16),
            pltpu.VMEM((CHUNKS * GROWS, 2 * ff), F32),
            pltpu.VMEM((CHUNKS * GROWS, width), BF16),
            pltpu.VMEM((CHUNKS * GROWS, ff), BF16),
            pltpu.VMEM((SIDE, SIDE, half, ff), BF16),
            pltpu.VMEM((SIDE, SIDE, half, ff), BF16),
            pltpu.VMEM((SIDE - 1, SIDE, half, ff), BF16),
            pltpu.VMEM((SIDE - 1, SIDE, half, ff), BF16),
            pltpu.VMEM((SIDE, half, ff), BF16),
            pltpu.VMEM((SIDE, half, ff), BF16),
            pltpu.VMEM((SIDE - 1, half, ff), BF16),
            pltpu.VMEM((SIDE - 1, half, ff), BF16),
            dma((5,)),
            dma((PEERS,)), dma((PEERS,)), dma((PEERS,)), dma((PEERS,)), dma((PEERS,)), dma((PEERS,)),
            dma((SIDE - 1,)), dma((SIDE - 1,)), dma((SIDE - 1,)), dma((SIDE - 1,)),
            dma((SIDE - 1,)), dma((SIDE - 1,)), dma((SIDE - 1,)), dma((SIDE - 1,)),
        ],
        compiler_params=pltpu.CompilerParams(
            collective_id=0, has_side_effects=True, vmem_limit_bytes=56 << 20
        ),
        cost_estimate=pl.CostEstimate(
            flops=3 * 10**9, bytes_accessed=8 * 10**6, transcendentals=250000
        ),
    )(
        expert_index, gate_weights, tokens, cotangent, w_gate[0], w_up[0], w_down[0]
    )
    return token_grad, down_t.T[None]


def solution(mesh):
    token_spec = P(("dp", "expert"), None)
    weight_spec = P("expert", None, None)
    return jax.shard_map(
        per_device,
        mesh=mesh,
        in_specs=(token_spec,) * 4 + (weight_spec,) * 3,
        out_specs=(token_spec, P("expert", None, "dp")),
        check_vma=False,
    )
```

time: 317 us -> 123 us (0.39)
  the two profiles are of different devices: /device:TPU:4 before, /device:TPU:16 now
where the time goes in v1:
time: 123 us; the launch traced here: 122 us
  Pallas kernels  116 us (94%)
  local copies, waits for them, and re-layouts  6.1 us (5%)
    pallas_call x1, Pallas kernels, per_device(): pl.pallas_call(body, out_shape=(jax.ShapeDtypeStruct((rows, width), BF16)...  116 us
    unnamed x4, local copies, waits for them, and re-layouts  6.1 us

profile of v1, /device:TPU:16, one launch (start us, length us, event | category | flops | bytes accessed | tf_op | source)
XLA Modules:
  0.0 122.4 jit_solution(4358469513912318640)
XLA Ops:
  0.6 1.4 %copy.10.gw_ref = bf16[128,2]{1,0:T(8,128)(2,1)} copy(bf16[128,2]{0,1:T(2,128)(2,1)} %param.9) | data formatting | bytes 1024 | tf_op args[2]
  2.0 1.4 %copy.9.ei_ref = s32[128,2]{1,0:T(8,128)} copy(s32[128,2]{0,1:T(2,128)} %param.8) | data formatting | bytes 2048 | tf_op args[1]
  3.4 115.7 %shard_map.86 = (bf16[128,2048]{1,0:T(8,128)(2,1)}, f32[32,384]{1,0:T(8,128)}) custom-call(s32[128,2]{1,0:T(8,128)} %copy.9.ei_ref, bf16[128,2]{1,0:T(8,128)(2,1)} %copy.10.gw_ref, bf16[128,2048]{1,0:T(8,128)(2,1)} %tok_hbm.1, bf16[128,2048]{1,0:T(8,128)(2,1)} %cot_hbm.1, bf16[2048,384]{1,0:T(8,128)(2,1)} %bitcast.7, bf16[2048,384]{1,0:T(8,128)(2,1)} %bitcast.8, ...), custom_call_target="tpu_custom_call" | custom-call | flops 3000000000 | bytes 8000000 | tf_op jit(solution)/shard_map/pallas_call | solution.py:323
  119.1 1.9 %copy.13 = bf16[128,2048]{1,0:T(8,128)(2,1)} copy(bf16[128,2048]{1,0:T(8,128)(2,1)} %get-tuple-element.8) | data formatting | bytes 1048576
  121.0 1.4 %copy.14 = f32[1,384,32]{1,2,0:T(8,128)} copy(f32[1,384,32]{1,2,0:T(8,128)} %bitcast.6) | data formatting | bytes 98304

commit v2 on v1

--- a/solution.py
+++ b/solution.py
@@ -83,16 +83,16 @@
         pl.semaphore_signal(barrier, inc=1, device_id=x_peer(k), device_id_type=MESH)
         pl.semaphore_signal(barrier, inc=1, device_id=z_peer(k), device_id_type=MESH)
 
-    lane_e = lax.broadcasted_iota(jnp.int32, (rows, PEERS), 1)
-    first = (ei_ref[:, 0:1] == lane_e).astype(F32)
-    second = (ei_ref[:, 1:2] == lane_e).astype(F32)
+    sub_e = lax.broadcasted_iota(jnp.int32, (PEERS, rows), 0)
+    first = (ei_ref[0:1, :] == sub_e).astype(F32)
+    second = (ei_ref[1:2, :] == sub_e).astype(F32)
     chosen = (first + second).astype(BF16)
     gates = gw_ref[...].astype(F32)
-    gates = (first * gates[:, 0:1] + second * gates[:, 1:2]).astype(BF16)
-    before = lax.broadcasted_iota(jnp.int32, (rows, rows), 1) < lax.broadcasted_iota(
-        jnp.int32, (rows, rows), 0
+    gates = (first * gates[0:1, :] + second * gates[1:2, :]).astype(BF16)
+    before = lax.broadcasted_iota(jnp.int32, (rows, rows), 0) < lax.broadcasted_iota(
+        jnp.int32, (rows, rows), 1
     )
-    place = dot(before.astype(F32).astype(BF16), chosen).astype(BF16)
+    place = dot(chosen, before.astype(F32).astype(BF16)).astype(BF16)
 
     def expert_at(block):
         along, other = offsets_of(block)
@@ -103,9 +103,9 @@
     pick = (
         expert_at(down_i // MAIN) == lax.broadcasted_iota(jnp.int32, (nrow, PEERS), 1)
     ).astype(F32).astype(BF16)
-    named = dot(pick, chosen, NT) > 0.5
-    at = dot(pick, place, NT).astype(jnp.int32)
-    gate_of = dot(pick, gates, NT)
+    named = dot(pick, chosen) > 0.5
+    at = dot(pick, place).astype(jnp.int32)
+    gate_of = dot(pick, gates)
     row_i = lax.broadcasted_iota(jnp.int32, (nrow, rows), 0)
     hit_main = jnp.where(named & (at == (row_i & (MAIN - 1))), 1.0, 0.0)
     hit_spare = jnp.where(named & (at == MAIN + (row_i & (SPARE - 1))), 1.0, 0.0)
@@ -116,27 +116,21 @@
     take_spare = [
         jnp.where(piece_i == g, hit_spare, 0.0).astype(BF16) for g in range(FOLD)
     ]
-    named_t = dot(chosen, pick, NT) > 0.5
-    at_t = dot(place, pick, NT).astype(jnp.int32)
-    col_i = lax.broadcasted_iota(jnp.int32, (rows, nrow), 1)
-    t_main[...] = jnp.where(named_t & (at_t == (col_i & (MAIN - 1))), 1.0, 0.0).astype(BF16)
-    t_spare[...] = jnp.where(
-        named_t & (at_t == MAIN + (col_i & (SPARE - 1))), 1.0, 0.0
-    ).astype(BF16)
-
-    def gather(source, out, scales):
+
+    def gather(source, out, scaled_by, lo, hi):
+        these = slice(lo * MAIN, hi * MAIN)
         for g in range(FOLD):
             cols = slice(g * fold, (g + 1) * fold)
-            got = dot(take_main, source[:, cols])
-            if scales is not None:
-                got = got * scales[0]
-            out[:, :, cols] = got.astype(BF16).reshape(PEERS, MAIN, fold)
-        got = dot(take_spare[0], source[:, 0:fold])
+            got = dot(take_main[these], source[:, cols])
+            if scaled_by is not None:
+                got = got * scaled_by[0][these]
+            out[lo:hi, :, cols] = got.astype(BF16).reshape(hi - lo, MAIN, fold)
+        got = dot(take_spare[0][these], source[:, 0:fold])
         for g in range(1, FOLD):
-            got = got + dot(take_spare[g], source[:, g * fold : (g + 1) * fold])
-        if scales is not None:
-            got = got * scales[1]
-        out[:, :, width:] = got.astype(BF16).reshape(PEERS, MAIN, fold)
+            got = got + dot(take_spare[g][these], source[:, g * fold : (g + 1) * fold])
+        if scaled_by is not None:
+            got = got * scaled_by[1][these]
+        out[lo:hi, :, width:] = got.astype(BF16).reshape(hi - lo, MAIN, fold)
 
     def move(slot, way, out, into, send, recv):
         return pltpu.make_async_remote_copy(
@@ -150,16 +144,31 @@
 
     own = PEERS - 1
     loads[0].wait()
-    gather(tok, x_out, None)
+    gather(tok, x_out, None, 0, GROUP)
     pl.semaphore_wait(barrier, PEERS - 1 + 2 * (SIDE - 1))
-    for slot in range(PEERS - 1):
+    for slot in range(GROUP):
+        move(slot, 1, x_out, x_in, xs_sem, xr_sem).start()
+    gather(tok, x_out, None, GROUP, PEERS)
+    for slot in range(GROUP, PEERS - 1):
         move(slot, 1, x_out, x_in, xs_sem, xr_sem).start()
     loads[1].wait()
-    gather(cot, c_out, (scale_main, scale_spare))
+    gather(cot, c_out, (scale_main, scale_spare), 0, PEERS)
     for slot in range(PEERS - 1):
         move(slot, 1, c_out, c_in, cs_sem, cr_sem).start()
     x_in[own] = x_out[own]
     c_in[own] = c_out[own]
+
+    pick_t = (
+        expert_at(lax.broadcasted_iota(jnp.int32, (PEERS, nrow), 1) // MAIN)
+        == lax.broadcasted_iota(jnp.int32, (PEERS, nrow), 0)
+    ).astype(F32).astype(BF16)
+    named_t = dot(chosen, pick_t, TN) > 0.5
+    at_t = dot(place, pick_t, TN).astype(jnp.int32)
+    col_i = lax.broadcasted_iota(jnp.int32, (rows, nrow), 1)
+    t_main[...] = jnp.where(named_t & (at_t == (col_i & (MAIN - 1))), 1.0, 0.0).astype(BF16)
+    t_spare[...] = jnp.where(
+        named_t & (at_t == MAIN + (col_i & (SPARE - 1))), 1.0, 0.0
+    ).astype(BF16)
 
     big_i = lax.broadcasted_iota(jnp.int32, (GS, GM), 1)
     small_i = lax.broadcasted_iota(jnp.int32, (GS, GM), 0)
@@ -203,11 +212,14 @@
     lax.fori_loop(0, CHUNKS, forward, 0)
     loads[4].wait()
 
-    def backward(chunk, carry):
+    def take(chunk, carry):
         for b in range(GROUP):
             wait_block(chunk * GROUP + b, 1, c_out, c_in, cs_sem, cr_sem)
+        unpack(c_in, chunk, scaled, pl.multiple_of(chunk * GROWS, GROWS))
+        return carry
+
+    def backward(chunk, carry):
         base = pl.multiple_of(chunk * GROWS, GROWS)
-        unpack(c_in, chunk, scaled, base)
         back = dot(scaled[pl.ds(base, GROWS), :], wd[...], NT)
         gate = pre[pl.ds(base, GROWS), 0:ff]
         up = pre[pl.ds(base, GROWS), ff:]
@@ -233,20 +245,10 @@
 
         return carry
 
-    lax.fori_loop(0, CHUNKS, backward, 0)
-    r_in[own] = r_out[own]
+    def both_steps(chunk, carry):
+        return backward(chunk, take(chunk, carry))
 
     half = part // (2 * SIDE)
-
-    def outer(zz, carry):
-        cols = pl.ds(pl.multiple_of(zz * part, part), part)
-        term = dot(scaled[:, cols], hidden[...], TN).astype(BF16).reshape(SIDE, 2, half, ff)
-        for xx in range(SIDE):
-            dt_a[xx, zz] = term[xx, 0]
-        dt_b[zz] = term[:, 1]
-        return carry
-
-    lax.fori_loop(0, SIDE, outer, 0)
 
     def share(k, peer, at_axis, out, into, send, recv):
         return pltpu.make_async_remote_copy(
@@ -258,10 +260,30 @@
             device_id_type=MESH,
         )
 
+    def outer(step, carry):
+        k = (4 - (step + 1) // 2) * (2 * (step & 1) - 1) & (SIDE - 1)
+        zz = (z + k) & (SIDE - 1)
+        cols = pl.ds(pl.multiple_of(zz * part, part), part)
+        term = dot(scaled[:, cols], hidden[...], TN).astype(BF16).reshape(SIDE, 2, half, ff)
+        for xx in range(SIDE):
+            dt_a[xx, zz] = term[xx, 0]
+        dt_b[zz] = term[:, 1]
+
+        @pl.when(step < SIDE - 1)
+        def _():
+            share(k, z_peer, z, dt_b, r_b, b1s, b1r).start()
+
+        return carry
+
     order = (4, 3, 5, 2, 6, 1, 7)
+    lax.fori_loop(0, CHUNKS // 2, both_steps, 0)
+    lax.fori_loop(CHUNKS // 2, CHUNKS, take, 0)
+    lax.fori_loop(0, SIDE, outer, 0)
     for k in order:
         share(k, x_peer, x, dt_a, r_a, a1s, a1r).start()
-        share(k, z_peer, z, dt_b, r_b, b1s, b1r).start()
+    lax.fori_loop(CHUNKS // 2, CHUNKS, backward, 0)
+    r_in[own] = r_out[own]
+
     for k in order:
         share(k, x_peer, x, dt_a, r_a, a1s, a1r).wait_recv()
     total = dt_a[x].astype(F32)
@@ -291,6 +313,14 @@
     dg_ref[half:, :] = total
 
     for slot in range(PEERS - 1):
+        move(slot, 1, x_out, x_in, xs_sem, xr_sem).wait_send()
+        move(slot, 1, c_out, c_in, cs_sem, cr_sem).wait_send()
+    for k in order:
+        share(k, x_peer, x, dt_a, r_a, a1s, a1r).wait_send()
+        share(k, z_peer, z, dt_b, r_b, b1s, b1r).wait_send()
+        share(k, z_peer, z, s_a, q_a, a2s, a2r).wait_send()
+        share(k, x_peer, x, s_b, q_b, b2s, b2r).wait_send()
+    for slot in range(PEERS - 1):
         move(slot, -1, r_out, r_in, rs_sem, rr_sem).wait_recv()
     col_piece = (lax.broadcasted_iota(jnp.int32, (rows, nrow), 1) & (MAIN - 1)) // SPARE
     spare = r_in[:, :, width:].reshape(nrow, fold)
@@ -301,14 +331,18 @@
         tg_ref[:, cols] = (dot(t_main[...], main) + dot(pick_g, spare)).astype(BF16)
 
     for slot in range(PEERS - 1):
-        move(slot, 1, x_out, x_in, xs_sem, xr_sem).wait_send()
-        move(slot, 1, c_out, c_in, cs_sem, cr_sem).wait_send()
         move(slot, -1, r_out, r_in, rs_sem, rr_sem).wait_send()
-    for k in order:
-        share(k, x_peer, x, dt_a, r_a, a1s, a1r).wait_send()
-        share(k, z_peer, z, dt_b, r_b, b1s, b1r).wait_send()
-        share(k, z_peer, z, s_a, q_a, a2s, a2r).wait_send()
-        share(k, x_peer, x, s_b, q_b, b2s, b2r).wait_send()
+
+
+def hand_over(tg_in, dg_in, tg_ref, dg_ref, sem):
+    copies = [
+        pltpu.make_async_copy(tg_in, tg_ref, sem.at[0]),
+        pltpu.make_async_copy(dg_in, dg_ref, sem.at[1]),
+    ]
+    for copy in copies:
+        copy.start()
+    for copy in copies:
+        copy.wait()
 
 
 def per_device(tokens, expert_index, gate_weights, cotangent, w_gate, w_up, w_down):
@@ -360,8 +394,18 @@
             flops=3 * 10**9, bytes_accessed=8 * 10**6, transcendentals=250000
         ),
     )(
-        expert_index, gate_weights, tokens, cotangent, w_gate[0], w_up[0], w_down[0]
+        expert_index.T, gate_weights.T, tokens, cotangent, w_gate[0], w_up[0], w_down[0]
     )
+    token_grad, down_t = pl.pallas_call(
+        hand_over,
+        out_shape=(
+            jax.ShapeDtypeStruct((rows, width), BF16),
+            jax.ShapeDtypeStruct((2 * half, ff), F32),
+        ),
+        in_specs=[vmem, vmem],
+        out_specs=(hbm, hbm),
+        scratch_shapes=[dma((2,))],
+    )(token_grad, down_t)
     return token_grad, down_t.T[None]
 
 

time: 123 us -> 113 us (0.919)
  the two profiles are of different devices: /device:TPU:16 before, /device:TPU:20 now
where the time goes in v2:
time: 113 us
  Pallas kernels  112 us (99%)
    pallas_call x1, Pallas kernels, per_device(): pl.pallas_call(body, out_shape=(jax.ShapeDtypeStruct((rows, width), BF16)...  110 us

profile of v2, /device:TPU:20, one launch (start us, length us, event | category | flops | bytes accessed | tf_op | source)
XLA Modules:
  0.0 112.9 jit_solution(6871893666436024167)
XLA Ops:
  0.6 110.4 %shard_map.86 = (bf16[128,2048]{1,0:T(8,128)(2,1)}, f32[32,384]{1,0:T(8,128)}) custom-call(s32[2,128]{1,0:T(2,128)} %bitcast.12, bf16[2,128]{1,0:T(2,128)(2,1)} %bitcast.13, bf16[128,2048]{1,0:T(8,128)(2,1)} %tok_hbm.1, bf16[128,2048]{1,0:T(8,128)(2,1)} %cot_hbm.1, bf16[2048,384]{1,0:T(8,128)(2,1)} %bitcast.8, bf16[2048,384]{1,0:T(8,128)(2,1)} %bitcast.9, ...), custom_call_target="tpu_custom_call" | custom-call | flops 3000000000 | bytes 8000000 | tf_op jit(solution)/shard_map/pallas_call | solution.py:357
  111.0 1.9 %shard_map.87 = (bf16[128,2048]{1,0:T(8,128)(2,1)}, f32[32,384]{1,0:T(8,128)}) custom-call(bf16[128,2048]{1,0:T(8,128)(2,1)} %get-tuple-element.6.tg_in, f32[32,384]{1,0:T(8,128)} %get-tuple-element.7.dg_in), custom_call_target="tpu_custom_call" | custom-call | tf_op jit(solution)/shard_map/pallas_call | solution.py:399

commit v3 on v2

--- a/solution.py
+++ b/solution.py
@@ -19,6 +19,7 @@
 FOLD = MAIN // SPARE
 GROUP = 4
 CHUNKS = PEERS // GROUP
+NEWS = 1
 GM = GROUP * MAIN
 GS = GROUP * SPARE
 GROWS = GM + GS
@@ -44,7 +45,7 @@
     t_main, t_spare, xs, pre, scaled, hidden,
     dt_a, dt_b, r_a, r_b, s_a, s_b, q_a, q_b,
     load_sem, xs_sem, xr_sem, cs_sem, cr_sem, rs_sem, rr_sem,
-    a1s, a1r, b1s, b1r, a2s, a2r, b2s, b2r,
+    a1s, a1r, b1s, b1r, a2s, a2r, b2s, b2r, ring_go, dp_go,
 ):
     width = tok.shape[1]
     rows = tok.shape[0]
@@ -77,11 +78,12 @@
         return (((z + k) & (SIDE - 1)) * SIDE + x, ex)
 
     barrier = pltpu.get_barrier_semaphore()
-    for slot in range(PEERS - 1):
-        pl.semaphore_signal(barrier, inc=1, device_id=target(slot, 1), device_id_type=MESH)
-    for k in range(1, SIDE):
-        pl.semaphore_signal(barrier, inc=1, device_id=x_peer(k), device_id_type=MESH)
-        pl.semaphore_signal(barrier, inc=1, device_id=z_peer(k), device_id_type=MESH)
+    for e in range(PEERS):
+        if e != NEWS:
+
+            @pl.when(ex != e)
+            def _():
+                pl.semaphore_signal(barrier, inc=1, device_id=(dp, e), device_id_type=MESH)
 
     sub_e = lax.broadcasted_iota(jnp.int32, (PEERS, rows), 0)
     first = (ei_ref[0:1, :] == sub_e).astype(F32)
@@ -143,14 +145,34 @@
         )
 
     own = PEERS - 1
+
     loads[0].wait()
     gather(tok, x_out, None, 0, GROUP)
-    pl.semaphore_wait(barrier, PEERS - 1 + 2 * (SIDE - 1))
+
+    @pl.when(ex != NEWS)
+    def _():
+        pl.semaphore_wait(barrier, PEERS - 1)
+
+    @pl.when(ex == 0)
+    def _():
+        pl.semaphore_signal(ring_go, inc=1, device_id=(dp, NEWS), device_id_type=MESH)
+
+    @pl.when(ex == NEWS)
+    def _():
+        pl.semaphore_wait(ring_go, 1)
+
     for slot in range(GROUP):
         move(slot, 1, x_out, x_in, xs_sem, xr_sem).start()
     gather(tok, x_out, None, GROUP, PEERS)
     for slot in range(GROUP, PEERS - 1):
         move(slot, 1, x_out, x_in, xs_sem, xr_sem).start()
+
+    @pl.when(ex == NEWS)
+    def _():
+        for k in range(1, SIDE):
+            pl.semaphore_signal(barrier, inc=1, device_id=x_peer(k), device_id_type=MESH)
+            pl.semaphore_signal(barrier, inc=1, device_id=z_peer(k), device_id_type=MESH)
+
     loads[1].wait()
     gather(cot, c_out, (scale_main, scale_spare), 0, PEERS)
     for slot in range(PEERS - 1):
@@ -210,6 +232,14 @@
         return carry
 
     lax.fori_loop(0, CHUNKS, forward, 0)
+
+    @pl.when(ex == NEWS)
+    def _():
+        pl.semaphore_wait(barrier, 2 * (SIDE - 1))
+        for e in range(PEERS):
+            if e != NEWS:
+                pl.semaphore_signal(dp_go, inc=1, device_id=(dp, e), device_id_type=MESH)
+
     loads[4].wait()
 
     def take(chunk, carry):
@@ -236,6 +266,9 @@
         r_out[pl.ds(chunk * GROUP, GROUP), :, pl.ds(width, fold)] = folded.astype(BF16).reshape(
             GROUP, MAIN, fold
         )
+        return carry
+
+    def send_back(chunk, carry):
         for b in range(GROUP):
             slot = chunk * GROUP + b
 
@@ -278,10 +311,18 @@
     order = (4, 3, 5, 2, 6, 1, 7)
     lax.fori_loop(0, CHUNKS // 2, both_steps, 0)
     lax.fori_loop(CHUNKS // 2, CHUNKS, take, 0)
+    lax.fori_loop(0, CHUNKS // 2, send_back, 0)
+
+    @pl.when(ex != NEWS)
+    def _():
+        pl.semaphore_wait(dp_go, 1)
+
     lax.fori_loop(0, SIDE, outer, 0)
     for k in order:
         share(k, x_peer, x, dt_a, r_a, a1s, a1r).start()
-    lax.fori_loop(CHUNKS // 2, CHUNKS, backward, 0)
+    lax.fori_loop(
+        CHUNKS // 2, CHUNKS, lambda chunk, carry: send_back(chunk, backward(chunk, carry)), 0
+    )
     r_in[own] = r_out[own]
 
     for k in order:
@@ -300,6 +341,19 @@
     s_b[...] = total.astype(BF16)
     for k in order:
         share(k, x_peer, x, s_b, q_b, b2s, b2r).start()
+    for slot in range(PEERS - 1):
+        move(slot, 1, x_out, x_in, xs_sem, xr_sem).wait_send()
+        move(slot, 1, c_out, c_in, cs_sem, cr_sem).wait_send()
+    for slot in range(PEERS - 1):
+        move(slot, -1, r_out, r_in, rs_sem, rr_sem).wait_recv()
+    col_piece = (lax.broadcasted_iota(jnp.int32, (rows, nrow), 1) & (MAIN - 1)) // SPARE
+    spare = r_in[:, :, width:].reshape(nrow, fold)
+    for g in range(FOLD):
+        cols = slice(g * fold, (g + 1) * fold)
+        main = r_in[:, :, cols].reshape(nrow, fold)
+        pick_g = jnp.where(col_piece == g, t_spare[...].astype(F32), 0.0).astype(BF16)
+        tg_ref[:, cols] = (dot(t_main[...], main) + dot(pick_g, spare)).astype(BF16)
+
     for k in order:
         share(k, z_peer, z, s_a, q_a, a2s, a2r).wait_recv()
         share(k, x_peer, x, s_b, q_b, b2s, b2r).wait_recv()
@@ -312,24 +366,11 @@
         total = total + q_b[k].astype(F32)
     dg_ref[half:, :] = total
 
-    for slot in range(PEERS - 1):
-        move(slot, 1, x_out, x_in, xs_sem, xr_sem).wait_send()
-        move(slot, 1, c_out, c_in, cs_sem, cr_sem).wait_send()
     for k in order:
         share(k, x_peer, x, dt_a, r_a, a1s, a1r).wait_send()
         share(k, z_peer, z, dt_b, r_b, b1s, b1r).wait_send()
         share(k, z_peer, z, s_a, q_a, a2s, a2r).wait_send()
         share(k, x_peer, x, s_b, q_b, b2s, b2r).wait_send()
-    for slot in range(PEERS - 1):
-        move(slot, -1, r_out, r_in, rs_sem, rr_sem).wait_recv()
-    col_piece = (lax.broadcasted_iota(jnp.int32, (rows, nrow), 1) & (MAIN - 1)) // SPARE
-    spare = r_in[:, :, width:].reshape(nrow, fold)
-    for g in range(FOLD):
-        cols = slice(g * fold, (g + 1) * fold)
-        main = r_in[:, :, cols].reshape(nrow, fold)
-        pick_g = jnp.where(col_piece == g, t_spare[...].astype(F32), 0.0).astype(BF16)
-        tg_ref[:, cols] = (dot(t_main[...], main) + dot(pick_g, spare)).astype(BF16)
-
     for slot in range(PEERS - 1):
         move(slot, -1, r_out, r_in, rs_sem, rr_sem).wait_send()
 
@@ -386,6 +427,7 @@
             dma((PEERS,)), dma((PEERS,)), dma((PEERS,)), dma((PEERS,)), dma((PEERS,)), dma((PEERS,)),
             dma((SIDE - 1,)), dma((SIDE - 1,)), dma((SIDE - 1,)), dma((SIDE - 1,)),
             dma((SIDE - 1,)), dma((SIDE - 1,)), dma((SIDE - 1,)), dma((SIDE - 1,)),
+            pltpu.SemaphoreType.REGULAR, pltpu.SemaphoreType.REGULAR,
         ],
         compiler_params=pltpu.CompilerParams(
             collective_id=0, has_side_effects=True, vmem_limit_bytes=56 << 20

time: 113 us -> 112 us (level)
  the two profiles are of different devices: /device:TPU:20 before, /device:TPU:16 now
where the time goes in v3:
time: 112 us
  Pallas kernels  111 us (99%)
    pallas_call x1, Pallas kernels, per_device(): pl.pallas_call(body, out_shape=(jax.ShapeDtypeStruct((rows, width), BF16)...  109 us

profile of v3, /device:TPU:16, one launch (start us, length us, event | category | flops | bytes accessed | tf_op | source)
XLA Modules:
  0.0 111.6 jit_solution(1151799371945193537)
XLA Ops:
  0.6 109.1 %shard_map.86 = (bf16[128,2048]{1,0:T(8,128)(2,1)}, f32[32,384]{1,0:T(8,128)}) custom-call(s32[2,128]{1,0:T(2,128)} %bitcast.12, bf16[2,128]{1,0:T(2,128)(2,1)} %bitcast.13, bf16[128,2048]{1,0:T(8,128)(2,1)} %tok_hbm.1, bf16[128,2048]{1,0:T(8,128)(2,1)} %cot_hbm.1, bf16[2048,384]{1,0:T(8,128)(2,1)} %bitcast.8, bf16[2048,384]{1,0:T(8,128)(2,1)} %bitcast.9, ...), custom_call_target="tpu_custom_call" | custom-call | flops 3000000000 | bytes 8000000 | tf_op jit(solution)/shard_map/pallas_call | solution.py:398
  109.7 1.9 %shard_map.87 = (bf16[128,2048]{1,0:T(8,128)(2,1)}, f32[32,384]{1,0:T(8,128)}) custom-call(bf16[128,2048]{1,0:T(8,128)(2,1)} %get-tuple-element.6.tg_in, f32[32,384]{1,0:T(8,128)} %get-tuple-element.7.dg_in), custom_call_target="tpu_custom_call" | custom-call | tf_op jit(solution)/shard_map/pallas_call | solution.py:441

commit v4 on v3

--- a/solution.py
+++ b/solution.py
@@ -45,7 +45,7 @@
     t_main, t_spare, xs, pre, scaled, hidden,
     dt_a, dt_b, r_a, r_b, s_a, s_b, q_a, q_b,
     load_sem, xs_sem, xr_sem, cs_sem, cr_sem, rs_sem, rr_sem,
-    a1s, a1r, b1s, b1r, a2s, a2r, b2s, b2r, ring_go, dp_go,
+    a1s, a1r, b1s, b1r, a2s, a2r, b2s, b2r, ring_go, dp_go, tg_out, leave_sem,
 ):
     width = tok.shape[1]
     rows = tok.shape[0]
@@ -346,13 +346,19 @@
         move(slot, 1, c_out, c_in, cs_sem, cr_sem).wait_send()
     for slot in range(PEERS - 1):
         move(slot, -1, r_out, r_in, rs_sem, rr_sem).wait_recv()
+
+    def leave(g):
+        cols = pl.ds(g * fold, fold)
+        return pltpu.make_async_copy(tg_out.at[:, cols], tg_ref.at[:, cols], leave_sem.at[g])
+
     col_piece = (lax.broadcasted_iota(jnp.int32, (rows, nrow), 1) & (MAIN - 1)) // SPARE
     spare = r_in[:, :, width:].reshape(nrow, fold)
     for g in range(FOLD):
         cols = slice(g * fold, (g + 1) * fold)
         main = r_in[:, :, cols].reshape(nrow, fold)
         pick_g = jnp.where(col_piece == g, t_spare[...].astype(F32), 0.0).astype(BF16)
-        tg_ref[:, cols] = (dot(t_main[...], main) + dot(pick_g, spare)).astype(BF16)
+        tg_out[:, cols] = (dot(t_main[...], main) + dot(pick_g, spare)).astype(BF16)
+        leave(g).start()
 
     for k in order:
         share(k, z_peer, z, s_a, q_a, a2s, a2r).wait_recv()
@@ -373,16 +379,25 @@
         share(k, x_peer, x, s_b, q_b, b2s, b2r).wait_send()
     for slot in range(PEERS - 1):
         move(slot, -1, r_out, r_in, rs_sem, rr_sem).wait_send()
-
-
-def hand_over(tg_in, dg_in, tg_ref, dg_ref, sem):
-    copies = [
-        pltpu.make_async_copy(tg_in, tg_ref, sem.at[0]),
-        pltpu.make_async_copy(dg_in, dg_ref, sem.at[1]),
-    ]
-    for copy in copies:
+    for g in range(FOLD):
+        leave(g).wait()
+
+
+def hand_over(tg_in, dg_in, tg_ref, dg_ref, tg_held, in_sem, out_sem):
+    step = tg_held.shape[0] // FOLD
+    coming, going = [], []
+    for g in range(FOLD):
+        some = pl.ds(g * step, step)
+        coming.append(pltpu.make_async_copy(tg_in.at[some], tg_held.at[some], in_sem.at[g]))
+        going.append(pltpu.make_async_copy(tg_held.at[some], tg_ref.at[some], out_sem.at[g]))
+    for copy in coming:
         copy.start()
-    for copy in copies:
+    going.append(pltpu.make_async_copy(dg_in, dg_ref, out_sem.at[FOLD]))
+    going[FOLD].start()
+    for g in range(FOLD):
+        coming[g].wait()
+        going[g].start()
+    for copy in going:
         copy.wait()
 
 
@@ -402,7 +417,7 @@
             jax.ShapeDtypeStruct((2 * half, ff), F32),
         ),
         in_specs=[vmem, vmem, hbm, hbm, hbm, hbm, hbm],
-        out_specs=(vmem, vmem),
+        out_specs=(hbm, vmem),
         scratch_shapes=[
             pltpu.VMEM((rows, width), BF16),
             pltpu.VMEM((rows, width), BF16),
@@ -428,6 +443,7 @@
             dma((SIDE - 1,)), dma((SIDE - 1,)), dma((SIDE - 1,)), dma((SIDE - 1,)),
             dma((SIDE - 1,)), dma((SIDE - 1,)), dma((SIDE - 1,)), dma((SIDE - 1,)),
             pltpu.SemaphoreType.REGULAR, pltpu.SemaphoreType.REGULAR,
+            pltpu.VMEM((rows, width), BF16), dma((FOLD,)),
         ],
         compiler_params=pltpu.CompilerParams(
             collective_id=0, has_side_effects=True, vmem_limit_bytes=56 << 20
@@ -444,9 +460,9 @@
             jax.ShapeDtypeStruct((rows, width), BF16),
             jax.ShapeDtypeStruct((2 * half, ff), F32),
         ),
-        in_specs=[vmem, vmem],
+        in_specs=[hbm, vmem],
         out_specs=(hbm, hbm),
-        scratch_shapes=[dma((2,))],
+        scratch_shapes=[pltpu.VMEM((rows, width), BF16), dma((FOLD,)), dma((FOLD + 1,))],
     )(token_grad, down_t)
     return token_grad, down_t.T[None]
 

time: 112 us -> 112 us (level)
  no operation moved by 1% of the time
where the time goes in v4:
time: 112 us
  Pallas kernels  112 us (100%)
    pallas_call x1, Pallas kernels, per_device(): pl.pallas_call(body, out_shape=(jax.ShapeDtypeStruct((rows, width), BF16)...  109 us
    pallas_call x1, Pallas kernels, per_device(): pl.pallas_call(hand_over, out_shape=(jax.ShapeDtypeStruct((rows, width),...  2.64 us

profile of v4, /device:TPU:16, one launch (start us, length us, event | category | flops | bytes accessed | tf_op | source)
XLA Modules:
  0.0 112.2 jit_solution(292969914464436798)
XLA Ops:
  0.6 108.9 %shard_map.86 = (bf16[128,2048]{1,0:T(8,128)(2,1)}, f32[32,384]{1,0:T(8,128)}) custom-call(s32[2,128]{1,0:T(2,128)} %bitcast.12, bf16[2,128]{1,0:T(2,128)(2,1)} %bitcast.13, bf16[128,2048]{1,0:T(8,128)(2,1)} %tok_hbm.1, bf16[128,2048]{1,0:T(8,128)(2,1)} %cot_hbm.1, bf16[2048,384]{1,0:T(8,128)(2,1)} %bitcast.8, bf16[2048,384]{1,0:T(8,128)(2,1)} %bitcast.9, ...), custom_call_target="tpu_custom_call" | custom-call | flops 3000000000 | bytes 8000000 | tf_op jit(solution)/shard_map/pallas_call | solution.py:413
  109.6 2.6 %shard_map.87 = (bf16[128,2048]{1,0:T(8,128)(2,1)}, f32[32,384]{1,0:T(8,128)}) custom-call(bf16[128,2048]{1,0:T(8,128)(2,1)} %get-tuple-element.6.tg_in, f32[32,384]{1,0:T(8,128)} %get-tuple-element.7.dg_in), custom_call_target="tpu_custom_call" | custom-call | tf_op jit(solution)/shard_map/pallas_call | solution.py:457
